TPU v7x, 32 devices: a whole 2x2x4 slice. The times are simulated.
32 devices in a mesh: sec: 4 (over z), col: 4 (over y, x), sect: 2 (over core).
Axes of the slice: x: 2, y: 2, z: 4, core: 2. Of those that a mesh axis runs over, the one named last changes fastest.
Arguments:
- transfer: float32 [16, 16, 2, 256, 256], P('sec', ('col', 'sect')), may hold values from -1 to 2
- trunc_ranks: int32 [16, 16, 2], P('sec', ('col', 'sect')), may hold values from 64 to 256
Outputs:
- gradient: float32 [16, 16, 2, 256, 256], P('sec', 'col', 'sect')
All inputs are finite; a program needn't handle non-finite values.
Results may differ from a plain program's by a relative error of at most 0.038.
Values sent between devices are 32-bit elements; how exact they have to be, the bound alone decides.
A program may use at most 192 MiB of HBM per device.

v0:
```python
import math

import jax
import jax.numpy as jnp
from jax import lax
from jax.sharding import PartitionSpec as P


def carried_in(part, axis, combine, identity, reverse):
    count = lax.axis_size(axis)
    place = lax.axis_index(axis)
    ahead = count - 1 - place if reverse else place
    gathered = lax.all_gather(part, axis)
    state = jnp.zeros_like(part) + jnp.asarray(identity, part.dtype)

    def one(lap, state):
        source = count - 1 - lap if reverse else lap
        return combine(state, lax.dynamic_index_in_dim(gathered, source, 0, False))

    return lax.fori_loop(0, ahead, one, state)


def product(former, latter):
    return jnp.einsum("...ik,...kj->...ij", former, latter, precision=lax.Precision.HIGHEST)


def flipped(matrix):
    return jnp.swapaxes(matrix, -1, -2)


def left_combine(earlier, latter):
    return product(earlier, latter)


def right_combine(earlier, latter):
    return product(latter, earlier)


def orthonormal(row_envs, trunc_ranks):
    bond_width = row_envs.shape[-1]
    unit_matrix = jnp.eye(bond_width, dtype=jnp.float32)
    kept_mask = (jnp.arange(bond_width, dtype=jnp.int32) < trunc_ranks[..., None]).astype(
        jnp.float32
    )
    truncated = (
        kept_mask[..., :, None] * row_envs * kept_mask[..., None, :]
        + unit_matrix * (1.0 - kept_mask)[..., None, :]
    )
    gram_matrix = product(flipped(truncated), truncated)
    lower_factor = jnp.linalg.cholesky(gram_matrix)
    solved = lax.linalg.triangular_solve(
        lower_factor, flipped(truncated), left_side=True, lower=True
    )
    return flipped(solved)


def column_sweeps(blocks):
    bond_width = blocks.shape[-1]
    by_column = jnp.moveaxis(blocks, 1, 0)
    unit_block = jnp.broadcast_to(jnp.eye(bond_width, dtype=jnp.float32), by_column.shape[1:])

    def sweep_left(running, factor):
        return (product(running, factor), running)

    def sweep_right(running, factor):
        return (product(factor, running), running)

    chip_total, inner_left = lax.scan(sweep_left, unit_block, by_column)
    _, inner_right = lax.scan(sweep_right, unit_block, by_column, reverse=True)
    return (chip_total, inner_left, inner_right, unit_block)


def finish_gradient(inner_left, inner_right, outer_left, outer_right):
    bond_width = inner_left.shape[-1]
    left_envs = product(outer_left[None], inner_left)
    right_envs = product(inner_right, outer_right[None])
    gradient = math.sqrt(bond_width) * flipped(product(right_envs, left_envs))
    return jnp.moveaxis(gradient, 0, 1)


def on_device(transfer, trunc_ranks):
    bond_width = transfer.shape[-1]
    unit_block = jnp.broadcast_to(jnp.eye(bond_width, dtype=jnp.float32), transfer.shape[1:])

    def absorb_down(running, factor):
        return (product(factor, running), running)

    def absorb_up(running, factor):
        return (product(running, factor), running)

    section_total, inner_above = lax.scan(absorb_down, unit_block, transfer)
    _, inner_below = lax.scan(absorb_up, unit_block, transfer, reverse=True)
    outer_above = carried_in(section_total, "sec", right_combine, unit_block, False)
    outer_below = carried_in(section_total, "sec", left_combine, unit_block, True)
    env_above = product(inner_above, outer_above[None])
    env_below = product(outer_below[None], inner_below)
    row_envs = flipped(product(env_above, env_below))
    blocks = orthonormal(row_envs, trunc_ranks)
    owned_blocks = lax.all_to_all(blocks, "sect", split_axis=2, concat_axis=1, tiled=True)
    chip_total, inner_left, inner_right, column_unit = column_sweeps(owned_blocks)
    outer_left = carried_in(chip_total, "col", left_combine, column_unit, False)
    outer_right = carried_in(chip_total, "col", right_combine, column_unit, True)
    result = finish_gradient(inner_left, inner_right, outer_left, outer_right)
    return result


def solution(mesh):
    in_specs = (P("sec", ("col", "sect"), None, None, None), P("sec", ("col", "sect"), None))
    out_specs = P("sec", "col", "sect", None, None)
    return jax.shard_map(
        on_device, mesh=mesh, in_specs=in_specs, out_specs=out_specs, check_vma=False
    )
```

profile of v0, /device:TPU:0, one launch (start us, length us, event | category | flops | bytes accessed | tf_op | source)
XLA Modules:
  0.0 1170.1 jit_solution(7672187761286546989)
XLA Ops:
  6.7 14.2 %while.111 = (s32[]{:T(128)}, f32[2,2,256,256]{3,2,1,0:T(8,128)S(1)}, f32[4,2,2,256,256]{4,3,2,1,0:T(8,128)}, f32[4,2,2,256,256]{4,3,2,1,0:T(8,128)}) while((s32[]{:T(128)}, f32[2,2,256,256]{3,2,1,0:T(8,128)S(1)}, f32[4,2,2,256,256]{4,3,2,1,0:T(8,128)}, f32[4,2,2,256,256]{4,3,2,1,0:T(8,128)}) %tuple.230), condition=%wide.region_3.4_spmd.clone, body=%wide.region_2.3_spmd.sunk.clone | while | flops 805306368 | bytes 7341109 | solution.py:91
  22.6 2.4 broadcast.130.clone
  25.0 17.2 %while.110 = (s32[]{:T(128)}, f32[2,2,256,256]{2,3,1,0:T(8,128)S(1)}, f32[4,2,2,256,256]{3,4,2,1,0:T(8,128)}, f32[4,2,2,256,256]{4,3,2,1,0:T(8,128)}) while((s32[]{:T(128)}, f32[2,2,256,256]{2,3,1,0:T(8,128)S(1)}, f32[4,2,2,256,256]{3,4,2,1,0:T(8,128)}, f32[4,2,2,256,256]{4,3,2,1,0:T(8,128)}) %tuple.263), condition=%wide.region_1.2_spmd.clone, body=%wide.region_0.1_spmd.sunk.clone | while | flops 805306368 | bytes 7340105 | solution.py:92
  26.1 3.1 convolution_bitcast_fusion.18
  30.4 3.2 convolution_bitcast_fusion.18
  34.8 3.1 convolution_bitcast_fusion.18
  39.1 3.1 convolution_bitcast_fusion.18
  42.2 63.4 %all-gather.5.cloned.1.call-done = f32[8,2,256,256]{3,2,1,0:T(8,128)} async-done(((f32[2,2,256,256]{3,2,1,0:T(8,128)}), f32[8,2,256,256]{3,2,1,0:T(8,128)}) %all-gather.5.cloned.1.call-update) | async-done | bytes 4194320 | tf_op jit(solution)/shard_map/all_gather | solution.py:13
  105.6 9.6 while.112
  105.7 3.1 convolution_bitcast_fusion.19
  108.9 3.1 convolution_bitcast_fusion.19
  112.1 3.1 convolution_bitcast_fusion.19
  115.8 5.8 fusion.70
  121.6 7.3 fusion.68
  128.9 6.1 bitcast_add_fusion
  135.0 10.2 fusion.41
  145.1 5.3 copy.167
  150.4 4.0 fusion.33
  156.5 187.6 %custom-call.16 = f32[4,2,2,128,128]{4,3,2,1,0:T(8,128)S(1)} custom-call(f32[4,2,2,128,128]{4,3,2,1,0:T(8,128)S(1)} %cholesky.119), custom_call_target="Cholesky" | custom-call | tf_op jit(solution)/shard_map/jit(cholesky)/cholesky | solution.py:50
  344.1 2.4 cholesky.115
  346.6 158.1 %custom-call.17 = f32[4,2,2,1,128,128]{4,5,3,2,1,0:T(8,128)} custom-call(f32[4,2,2,1,128,128]{5,4,3,2,1,0:T(8,128)S(1)} %select_bitcast_fusion), custom_call_target="InvertDiagBlocksLowerTriangular" | custom-call | tf_op jit(solution)/shard_map/jit(cholesky)/cholesky | solution.py:50
  504.7 3.8 constant_dynamic-update-slice_fusion.1
  508.5 4.5 convolution_subtract_fusion
  513.0 188.3 %custom-call.18 = f32[4,2,2,128,128]{4,3,2,1,0:T(8,128)S(1)} custom-call(f32[4,2,2,128,128]{4,3,2,1,0:T(8,128)} %convolution_subtract_fusion), custom_call_target="Cholesky" | custom-call | tf_op jit(solution)/shard_map/jit(cholesky)/cholesky | solution.py:50
  703.3 4.8 select_select_fusion
  708.2 9.8 while.118
  708.8 4.4 bitcast_dynamic-update-slice_fusion.19
  713.9 4.0 bitcast_dynamic-update-slice_fusion.19
  717.9 315.5 %custom-call.19 = f32[4,2,2,2,128,128]{4,5,3,2,1,0:T(8,128)S(1)} custom-call(f32[4,2,2,2,128,128]{5,4,3,2,1,0:T(8,128)} %bitcast.261), custom_call_target="InvertDiagBlocksLowerTriangular" | custom-call | tf_op jit(solution)/shard_map/triangular_solve | solution.py:51
  1033.5 3.7 fusion.55
  1037.2 5.0 fusion.61
  1045.0 8.6 all_to_all.18
  1053.6 5.3 copy.180
  1059.0 16.9 %while.114 = (s32[]{:T(128)}, f32[4,1,256,256]{2,3,0,1:T(8,128)S(1)}, f32[4,4,1,256,256]{3,4,1,2,0:T(8,128)}, f32[4,4,1,256,256]{4,3,0,1,2:T(8,128)}) while((s32[]{:T(128)}, f32[4,1,256,256]{2,3,0,1:T(8,128)S(1)}, f32[4,4,1,256,256]{3,4,1,2,0:T(8,128)}, f32[4,4,1,256,256]{4,3,0,1,2:T(8,128)}) %tuple.261), condition=%wide.region_13.14_spmd.clone, body=%wide.region_12.13_spmd.sunk.clone | while | flops 805306368 | bytes 7341109 | solution.py:68
  1060.1 3.1 convolution_bitcast_fusion.20
  1064.4 3.1 convolution_bitcast_fusion.20
  1068.6 3.1 convolution_bitcast_fusion.20
  1072.8 3.1 convolution_bitcast_fusion.20
  1077.4 2.4 broadcast.129
  1079.8 14.4 %while.116 = (s32[]{:T(128)}, f32[4,1,256,256]{3,2,0,1:T(8,128)S(1)}, f32[4,4,1,256,256]{4,3,1,2,0:T(8,128)}, f32[4,4,1,256,256]{4,3,0,1,2:T(8,128)}) while((s32[]{:T(128)}, f32[4,1,256,256]{3,2,0,1:T(8,128)S(1)}, f32[4,4,1,256,256]{4,3,1,2,0:T(8,128)}, f32[4,4,1,256,256]{4,3,0,1,2:T(8,128)}) %tuple.262), condition=%wide.region_17.18_spmd.clone, body=%wide.region_16.17_spmd.sunk.clone | while | flops 805306368 | bytes 7340105 | solution.py:69
  1081.0 2.4 convolution_bitcast_fusion.22
  1084.6 2.5 convolution_bitcast_fusion.22
  1094.3 34.1 %all-gather.7.cloned.1.call-done = f32[16,1,256,256]{3,2,1,0:T(8,128)} async-done(((f32[4,1,256,256]{3,2,1,0:T(8,128)}), f32[16,1,256,256]{3,2,1,0:T(8,128)}) %all-gather.7.cloned.1.call-update) | async-done | bytes 4194320 | tf_op jit(solution)/shard_map/all_gather | solution.py:13
  1128.5 7.5 while.115
  1136.1 9.0 fusion.44
  1145.0 4.3 fusion.47
  1149.4 8.5 multiply_bitcast_fusion
  1157.9 5.2 copy.195
  (103 shorter events, 52.5 us)
Async XLA Ops:
  6.5 99.0 %all-gather.5.cloned.1.call-start = ((), (), s32[]{:S(2)}) async-start(), calls=%async_computation.1 | async-start | bytes 5242880 | tf_op jit(solution)/shard_map/all_gather | solution.py:13
  6.7 15.5 %copy-start.5 = (s32[4,2,2]{0,2,1:T(2,128)S(1)}, s32[4,2,2]{0,2,1:T(2,128)}, u32[]{:S(2)}) copy-start(s32[4,2,2]{0,2,1:T(2,128)} %param.19) | copy-start | bytes 196
  20.9 1.0 copy-start
  21.9 1106.5 %all-gather.7.cloned.1.call-start = ((), (), s32[]{:S(2)}) async-start(), calls=%async_computation.2 | async-start | bytes 5242880 | tf_op jit(solution)/shard_map/all_gather | solution.py:13
  115.8 5.8 copy-start.3
  154.5 2.0 copy-start.2
  1033.5 8.8 copy-start.1
  1136.1 9.0 copy-start.4
Sparse Core Ops, SparseCore 0:
  22.0 83.4 all-gather.4
  1077.5 50.8 all-gather.6
where the time goes:
time: 1180 us; the launch traced here: 1170 us
  other arithmetic  861 us (73%)
  matrix products  130 us (11%)
  waiting for transfers between devices  97.5 us (8%)
  local copies, waits for them, and re-layouts  57.6 us (5%)
  between operations  14 us (1%)
    another operation x9, other arithmetic, orthonormal(): lower_factor = jnp.linalg.cholesky(gram_matrix)  536 us
    another operation x4, other arithmetic, orthonormal(): lax.linalg.triangular_solve(lower_factor, flipped(truncated), left_side=T...  320 us
    dot_general x29, matrix products, product(): jnp.einsum('...ik,...kj->...ij', former, latter, precision=lax.Precision....  111 us
    all_gather x2, waiting for transfers between devices, carried_in(): gathered = lax.all_gather(part, axis)  97.5 us
  transfers between devices with their start and end apart: 2, of which 2 were waited for; matrix products, arithmetic and copies ran while one was open for 3% of the time, Pallas kernels for 0%

commit v1 on v0

v1 whole, which is shorter than its diff:
```python
import functools
import math

import jax
import jax.numpy as jnp
from jax import lax
from jax.experimental import pallas as pl
from jax.experimental.pallas import tpu as pltpu
from jax.sharding import PartitionSpec as P

PANEL = 32
PACK = 128 // PANEL


def product(former, latter):
    return jnp.einsum("...ik,...kj->...ij", former, latter, precision=lax.Precision.HIGHEST)


def split3(value):
    first = value.astype(jnp.bfloat16)
    rest = value - first.astype(jnp.float32)
    second = rest.astype(jnp.bfloat16)
    third = (rest - second.astype(jnp.float32)).astype(jnp.bfloat16)
    return first, second, third


def stack_left(value, axis):
    a, b, c = split3(value)
    return jnp.concatenate([a, a, b, a, b, c], axis=axis)


def stack_right(value, axis):
    a, b, c = split3(value)
    return jnp.concatenate([a, b, a, c, b, a], axis=axis)


def panel_inverse(groups):
    lane = lax.broadcasted_iota(jnp.int32, (8, 128), 1)
    sub = lax.broadcasted_iota(jnp.int32, (8, 128), 0)
    local = lane % PANEL
    base = lane - local
    tiles = PANEL // 8
    work = [[g[8 * r : 8 * r + 8] for r in range(tiles)] for g in groups]
    inv = [
        [jnp.where(local == sub + 8 * r, 1.0, 0.0).astype(jnp.float32) for r in range(tiles)]
        for _ in groups
    ]
    for k in range(PANEL):
        own, at = divmod(k, 8)
        index = base + k
        for a, w in zip(work, inv):
            cols = [
                jnp.take_along_axis(a[r], index, axis=1, mode="promise_in_bounds")
                for r in range(own, tiles)
            ]
            pivot = cols[0][at : at + 1]
            recip = 1.0 / pivot
            row_a = a[own][at : at + 1] * recip
            row_w = w[own][at : at + 1] * recip
            scale = lax.rsqrt(pivot)
            for r in range(own, tiles):
                m = cols[r - own]
                if r == own:
                    m = jnp.where(sub > at, m, 0.0)
                a[r] = a[r] - m * row_a
                w[r] = w[r] - m * row_w
            w[own] = w[own] * jnp.where(sub == at, scale, 1.0)
    return [jnp.concatenate(w, axis=0) for w in inv]


def orthonormal_kernel(rank_ref, env_ref, out_ref, gram_ref, inv_ref):
    count, width, _ = env_ref.shape

    def start(m, carry):
        rank = rank_ref[m]
        row = lax.broadcasted_iota(jnp.int32, (width, width), 0)
        col = lax.broadcasted_iota(jnp.int32, (width, width), 1)
        kept = jnp.logical_and(row < rank, col < rank)
        unit = jnp.where(jnp.logical_and(row == col, row >= rank), 1.0, 0.0)
        value = jnp.where(kept, env_ref[m], unit)
        out_ref[m] = value
        gram_ref[m] = lax.dot_general(
            value,
            value,
            (((1,), (1,)), ((), ())),
            precision=lax.Precision.HIGHEST,
            preferred_element_type=jnp.float32,
        )
        return carry

    lax.fori_loop(0, count, start, 0)

    for p in range(width // PANEL):
        lo, hi = p * PANEL, (p + 1) * PANEL
        edge = lo // 128 * 128
        groups = [
            jnp.concatenate(
                [gram_ref[g * PACK + i, lo:hi, edge : edge + 128][:, lo - edge : hi - edge] for i in range(PACK)],
                axis=1,
            )
            for g in range(count // PACK)
        ]
        for g, packed in enumerate(panel_inverse(groups)):
            for i in range(PACK):
                inv_ref[g * PACK + i] = packed[:, i * PANEL : (i + 1) * PANEL]

        def update(m, carry):
            factor = stack_left(inv_ref[m], 1)
            rows_g = stack_right(gram_ref[m, lo:hi, edge:], 0)
            rows_r = stack_right(out_ref[m, lo:hi, :], 0)
            upper = jnp.dot(factor, rows_g, preferred_element_type=jnp.float32)
            done = jnp.dot(factor, rows_r, preferred_element_type=jnp.float32)
            out_ref[m, lo:hi, :] = done
            if hi < width:
                low = stack_left(upper, 0)
                low = low[:, (hi // 128 * 128) - edge :]
                skip = hi % 128
                first = hi // 128 * 128
                contract = (((0,), (0,)), ((), ()))
                tail_r = lax.dot_general(
                    low, stack_right(done, 0), contract, preferred_element_type=jnp.float32
                )
                tail_g = lax.dot_general(
                    low,
                    stack_right(upper, 0)[:, first - edge :],
                    contract,
                    preferred_element_type=jnp.float32,
                )
                out_ref[m, hi:, :] = out_ref[m, hi:, :] - tail_r[skip:]
                gram_ref[m, hi:, first:] = gram_ref[m, hi:, first:] - tail_g[skip:]
            return carry

        lax.fori_loop(0, count, update, 0)


def orthonormal(envs, ranks):
    count, width, _ = envs.shape
    vmem = pl.BlockSpec(memory_space=pltpu.VMEM)
    return pl.pallas_call(
        orthonormal_kernel,
        out_shape=jax.ShapeDtypeStruct(envs.shape, jnp.float32),
        in_specs=[pl.BlockSpec(memory_space=pltpu.SMEM), vmem],
        out_specs=vmem,
        scratch_shapes=[
            pltpu.VMEM((count, width, width), jnp.float32),
            pltpu.VMEM((count, PANEL, PANEL), jnp.float32),
        ],
        compiler_params=pltpu.CompilerParams(vmem_limit_bytes=40 * 2**20),
    )(ranks, envs)


def around(parts, axis):
    n = len(parts)
    above = [None, parts[0]]
    for r in range(1, n):
        above.append(product(parts[r], above[-1]))
    below = [None, parts[n - 1]]
    for r in range(n - 2, 0, -1):
        below.append(product(below[-1], parts[r]))
    below = below[::-1]
    total = above[n]
    devices = lax.axis_size(axis)
    me = lax.axis_index(axis)
    gathered = lax.all_gather(total, axis)
    middle = lax.dynamic_index_in_dim(gathered, (me + devices - 1) % devices, 0, False)
    for k in range(2, devices):
        other = lax.dynamic_index_in_dim(gathered, (me + devices - k) % devices, 0, False)
        middle = product(middle, other)
    result = []
    for r in range(n):
        value = middle
        if r:
            value = product(above[r], value)
        if r < n - 1:
            value = product(value, below[r])
        result.append(value)
    return result


def on_device(transfer, trunc_ranks):
    rows, cols, sectors, width, _ = transfer.shape
    envs = jnp.stack(around([transfer[r] for r in range(rows)], "sec"))
    blocks = orthonormal(envs.reshape(-1, width, width), trunc_ranks.reshape(-1))
    blocks = blocks.reshape(transfer.shape)
    owned = lax.all_to_all(blocks, "sect", split_axis=2, concat_axis=1, tiled=True)
    result = around([owned[:, c] for c in range(owned.shape[1])], "col")
    return math.sqrt(width) * jnp.stack(result, axis=1)


def solution(mesh):
    in_specs = (P("sec", ("col", "sect"), None, None, None), P("sec", ("col", "sect"), None))
    out_specs = P("sec", "col", "sect", None, None)
    return jax.shard_map(
        on_device, mesh=mesh, in_specs=in_specs, out_specs=out_specs, check_vma=False
    )
```

time: 1180 us -> 285 us (0.24)
  other arithmetic: 861 us -> 0.79 us
  Pallas kernels: 0 us -> 81.1 us
  matrix products: 130 us -> 49.8 us
  local copies, waits for them, and re-layouts: 57.6 us -> 4.81 us
  waiting for transfers between devices: 97.5 us -> 122 us
    another operation x15 -> x1, other arithmetic: 856 us -> 0.45 us  [on_device(): envs = jnp.stack(around([transfer[r] for r in range(rows)], 'sec'))]
    pallas_call x0 -> x1, Pallas kernels: none -> 81.1 us  [orthonormal(): pl.pallas_call(orthonormal_kernel, out_shape=jax.ShapeDtypeStruct(envs.sh...]
    dot_general x29 -> x26, matrix products: 111 us -> 49.8 us  [product(): jnp.einsum('...ik,...kj->...ij', former, latter, precision=lax.Precision....]
    all_gather x2, waiting for transfers between devices: 97.5 us -> 122 us  [around(): gathered = lax.all_gather(total, axis)]
    another operation x5 -> x0, matrix products: 19.1 us -> none  [the longest x3 10.8 us: orthonormal(): lax.linalg.triangular_solve(lower_factor, flipped(truncated), left_side=T...]
    another operation x12 -> x0, local copies, waits for them, and re-layouts: 17.3 us -> none
    dynamic_update_slice x16 -> x0, local copies, waits for them, and re-layouts: 17.1 us -> none  [the longest x8 8.62 us: on_device(): section_total, inner_above = lax.scan(absorb_down, unit_block, transfer)]
  transfers between devices with their start and end apart: 2 -> 2, of which waited for: 2 -> 2; matrix products, arithmetic and copies ran while one was open for 3% -> 4% of each run, Pallas kernels for 0% -> 0%
where the time goes in v1:
time: 285 us; the launch traced here: 280 us
  waiting for transfers between devices  122 us (43%)
  Pallas kernels  81.1 us (28%)
  matrix products  49.8 us (17%)
  between operations  14 us (5%)
  blocking collectives  7.1 us (2%)
  local copies, waits for them, and re-layouts  4.81 us (2%)
    all_gather x2, waiting for transfers between devices, around(): gathered = lax.all_gather(total, axis)  122 us
    pallas_call x1, Pallas kernels, orthonormal(): pl.pallas_call(orthonormal_kernel, out_shape=jax.ShapeDtypeStruct(envs.sh...  81.1 us
    dot_general x26, matrix products, product(): jnp.einsum('...ik,...kj->...ij', former, latter, precision=lax.Precision....  49.8 us
    all_to_all x1, blocking collectives, on_device(): lax.all_to_all(blocks, 'sect', split_axis=2, concat_axis=1, tiled=True)  7.1 us
  transfers between devices with their start and end apart: 2, of which 2 were waited for; matrix products, arithmetic and copies ran while one was open for 4% of the time, Pallas kernels for 0%

profile of v1, /device:TPU:0, one launch (start us, length us, event | category | flops | bytes accessed | tf_op | source)
XLA Modules:
  0.0 280.3 jit_solution(8710101134655901738)
XLA Ops:
  6.5 2.7 fusion.19
  9.2 0.0 copy-start.5
  9.2 3.1 %fusion.15 = f32[2,2,256,256]{3,2,1,0:T(8,128)S(1)} fusion(f32[2,2,256,256]{3,2,1,0:T(8,128)S(1)} %fusion.19, f32[4,2,2,256,256]{4,3,2,1,0:T(8,128)} %param.2), kind=kOutput, calls=%fused_computation.30 | convolution fusion | flops 805306368 | bytes 3145728 | tf_op jit(solution)/shard_map/...ik,...kj->...ij/dot_general | solution.py:16
  12.3 2.4 convolution_bitcast_fusion.8
  14.7 1.3 copy.17
  16.0 0.0 all-gather.5.cloned.1.call-update
  16.0 0.2 all-gather.7.cloned.1.call-start
  16.3 0.0 copy-done.5
  16.3 0.1 copy.15
  16.4 0.1 reshape.161.rank_ref
  16.5 2.7 fusion.11
  19.2 3.3 %fusion.21 = f32[2,2,256,256]{3,2,1,0:T(8,128)} fusion(f32[2,2,256,256]{3,2,1,0:T(8,128)S(1)} %fusion.11, f32[4,2,2,256,256]{4,3,2,1,0:T(8,128)} %param.2), kind=kOutput, calls=%fused_computation.36 | convolution fusion | flops 805306368 | bytes 3145728 | tf_op jit(solution)/shard_map/...ik,...kj->...ij/dot_general | solution.py:16
  22.5 77.1 %all-gather.5.cloned.1.call-done = f32[8,2,256,256]{3,2,1,0:T(8,128)} async-done(((f32[2,2,256,256]{3,2,1,0:T(8,128)}), f32[8,2,256,256]{3,2,1,0:T(8,128)}) %all-gather.5.cloned.1.call-update) | async-done | bytes 4194320 | tf_op jit(solution)/shard_map/all_gather | solution.py:164
  99.6 2.7 fusion.7
  102.3 0.0 copy-start.2
  102.3 2.5 fusion.5
  104.9 1.9 convolution_bitcast_fusion.4
  106.7 1.1 fusion.49
  107.9 0.0 copy-done.2
  107.9 0.0 copy-start.4
  107.9 1.1 fusion.17
  109.1 1.1 convolution_bitcast_fusion.5
  110.2 1.1 convolution_bitcast_fusion.6
  111.4 1.4 convolution_bitcast_fusion.7
  112.7 0.4 pad_maximum_fusion
  113.2 81.1 %shard_map.28 = f32[16,256,256]{2,1,0:T(8,128)S(1)} custom-call(s32[16]{0:T(128)S(1)} %reshape.161.rank_ref, f32[16,256,256]{2,1,0:T(8,128)S(1)} %bitcast.115), custom_call_target="tpu_custom_call" | custom-call | tf_op jit(solution)/shard_map/pallas_call | solution.py:139
  194.3 0.5 copy.21
  194.8 7.1 %all_to_all.18 = f32[4,2,2,256,256]{4,3,1,0,2:T(8,128)S(1)} all-to-all(f32[4,2,2,256,256]{4,3,1,0,2:T(8,128)S(1)} %copy.21), channel_id=1, replica_groups=mesh['sec'=4,'col'=4,'sect'=2] {'sect'}, dimensions={2} | all-to-all | bytes 8388608 | tf_op jit(solution)/shard_map/all_to_all | solution.py:185
  201.9 0.4 copy.22
  202.3 0.0 copy-start
  202.3 1.1 fusion.33
  203.5 1.1 fusion.31
  204.6 2.1 fusion.41
  206.7 0.0 all-gather.7.cloned.1.call-update
  206.8 2.7 fusion.30
  209.5 3.4 %fusion.32 = f32[4,256,256]{2,1,0:T(8,128)} fusion(f32[4,256,256]{2,1,0:T(8,128)S(1)} %fusion.30, f32[4,4,1,256,256]{4,3,0,2,1:T(8,128)} %bitcast.121), kind=kOutput, calls=%fused_computation.47 | convolution fusion | flops 805306368 | bytes 3145728 | tf_op jit(solution)/shard_map/...ik,...kj->...ij/dot_general | solution.py:16
  212.9 45.3 %all-gather.7.cloned.1.call-done = f32[16,256,256]{2,1,0:T(8,128)} async-done(((f32[4,256,256]{2,1,0:T(8,128)}), f32[16,256,256]{2,1,0:T(8,128)}) %all-gather.7.cloned.1.call-update) | async-done | bytes 4194320 | tf_op jit(solution)/shard_map/all_gather | solution.py:164
  258.2 2.7 fusion.2
  260.8 0.0 copy-start.1
  260.8 2.5 fusion
  263.4 1.1 convolution_bitcast_fusion
  264.5 1.1 fusion.50
  265.7 1.3 fusion.34
  267.0 1.1 convolution_bitcast_fusion.1
  268.2 1.1 convolution_bitcast_fusion.2
  269.3 1.1 convolution_bitcast_fusion.3
  270.5 0.3 maximum_multiply_fusion
  270.8 2.4 copy.26
  (6 shorter events, 0.0 us)
Async XLA Ops:
  6.5 93.1 %all-gather.5.cloned.1.call-start = ((), (), s32[]{:S(2)}) async-start(), calls=%async_computation.1 | async-start | bytes 5242880 | tf_op jit(solution)/shard_map/all_gather | solution.py:164
  9.2 7.1 %copy-start.5 = (s32[4,2,2]{0,2,1:T(2,128)S(1)}, s32[4,2,2]{0,2,1:T(2,128)}, u32[]{:S(2)}) copy-start(s32[4,2,2]{0,2,1:T(2,128)} %param.3) | copy-start | bytes 196
  16.0 242.1 %all-gather.7.cloned.1.call-start = ((), (), s32[]{:S(2)}) async-start(), calls=%async_computation.2 | async-start | bytes 5242880 | tf_op jit(solution)/shard_map/all_gather | solution.py:164
  102.3 5.6 %copy-start.2 = (f32[4,2,2,256,256]{4,3,2,1,0:T(8,128)S(1)}, f32[4,2,2,256,256]{4,3,2,1,0:T(8,128)}, u32[]{:S(2)}) copy-start(f32[4,2,2,256,256]{4,3,2,1,0:T(8,128)} %param.2) | copy-start | bytes 12582916
  107.9 3.5 %copy-start.4 = (f32[2,2,256,256]{3,2,1,0:T(8,128)S(1)}, f32[2,2,256,256]{3,2,1,0:T(8,128)}, u32[]{:S(2)}) copy-start(f32[2,2,256,256]{3,2,1,0:T(8,128)} %fusion.21) | copy-start | bytes 3145732
  202.3 2.3 copy-start
  260.8 4.8 %copy-start.1 = (f32[4,2,2,1,256,256]{5,4,0,2,1,3:T(8,128)S(1)}, f32[4,2,2,1,256,256]{5,4,0,2,1,3:T(8,128)}, u32[]{:S(2)}) copy-start(f32[4,2,2,1,256,256]{5,4,0,2,1,3:T(8,128)} %copy-done) | copy-start | bytes 12582916
  265.7 3.7 %copy-start.3 = (f32[4,256,256]{2,1,0:T(8,128)S(1)}, f32[4,256,256]{2,1,0:T(8,128)}, u32[]{:S(2)}) copy-start(f32[4,256,256]{2,1,0:T(8,128)} %fusion.32) | copy-start | bytes 3145732
Sparse Core Ops, SparseCore 0:
  16.1 83.4 all-gather.4
  206.9 51.2 all-gather.6
